TPU v7x, 32 devices: a whole 2x2x4 slice. The times are simulated.
32 devices in a mesh: dom: 8 (over z, x), sub: 4 (over y, core).
Axes of the slice: x: 2, y: 2, z: 4, core: 2. Of those that a mesh axis runs over, the one named last changes fastest.
Arguments:
- excitation: bfloat16 [8, 1536, 64], P('dom', 'sub'), may hold values from -6 to 6
- local_inverse: bfloat16 [8, 1536, 1536], P('dom', 'sub'), as said below
- aggregation: bfloat16 [8, 1024, 1536], P('dom', None, 'sub'), may hold values from -0.15625 to 0.15625
- disaggregation: bfloat16 [8, 1536, 1024], P('dom', 'sub'), may hold values from -0.1875 to 0.1875
- translation: float32 [8, 6, 2, 512], P('dom'), may hold values from -1.5 to 1.5
- partners: int32 [8, 6], P('dom'), may hold values from 0 to 7, as said below
- list_counts: int32 [8], P('dom'), may hold values from 2 to 6
- sweep_order: int32 [8], replicated, may hold values from 0 to 7, as said below
Outputs:
- currents: float32 [8, 1536, 64], P('dom', 'sub')
Inputs may be any that keep to these rules, and one draw needn't show every extreme that they name: `partners`: row d names 6 different subdomains, none equal to d; only its first list_counts[d] slots are used. `local_inverse`: each subdomain's matrix is the identity plus independent entries of spread 0.6 / sqrt(1536). `sweep_order`: every subdomain has a position of its own.
All inputs are finite; a program needn't handle non-finite values.
Results may differ from a plain program's by a relative error of at most 0.03.
Values may be sent and summed in bfloat16 or wider, within the bound.
A program may use at most 64 MiB of HBM per device.

v0:
```python
import jax
import jax.numpy as jnp
from jax import lax
from jax.sharding import PartitionSpec as P

SEGMENTS = 8


CONTRACT_FIRST = (((0,), (1,)), ((), ()))
CONTRACT_LAST = (((1,), (1,)), ((), ()))


def rotate(real_weight, imag_weight, pattern):
    samples = real_weight.shape[-1]
    values = pattern.astype(jnp.float32)
    real_part = values[..., :samples]
    imag_part = values[..., samples:]
    return jnp.concatenate(
        [
            real_weight * real_part - imag_weight * imag_part,
            real_weight * imag_part + imag_weight * real_part,
        ],
        axis=-1,
    )


def local(
    excitation,
    local_inverse,
    aggregation,
    disaggregation,
    translation,
    partners,
    list_counts,
    sweep_order,
):
    excite_rows = excitation[0]
    inverse_rows = local_inverse[0]
    agg_columns = aggregation[0]
    disagg_rows = disaggregation[0]
    trans_rows = translation[0]
    partner_row = partners[0]

    def apply_inverse(shard_rows):
        return jnp.dot(inverse_rows, shard_rows, preferred_element_type=jnp.float32)

    solved = apply_inverse(lax.all_gather(excite_rows, "sub", axis=0, tiled=True))
    solved_half = solved.astype(jnp.bfloat16)
    incident = lax.psum_scatter(
        lax.dot_general(
            solved_half, agg_columns, CONTRACT_FIRST, preferred_element_type=jnp.float32
        ).astype(jnp.bfloat16),
        "sub",
        scatter_dimension=0,
        tiled=True,
    ).astype(jnp.float32)
    spread = apply_inverse(lax.all_gather(disagg_rows, "sub", axis=0, tiled=True))
    spread_half = spread.astype(jnp.bfloat16)
    partial_map = lax.dot_general(
        spread_half, agg_columns, CONTRACT_FIRST, preferred_element_type=jnp.float32
    )
    coupling = lax.psum(partial_map.astype(jnp.bfloat16), "sub")
    domains = sweep_order.shape[0]
    segment_of = sweep_order * SEGMENTS // domains
    own_index = lax.axis_index("dom")
    my_segment = segment_of[own_index]
    slot_live = jnp.arange(partner_row.shape[0], dtype=jnp.int32) < list_counts[0]
    domain_ids = jnp.arange(domains, dtype=jnp.int32)
    incoming = jnp.zeros(incident.shape, jnp.float32)
    for segment_k in range(SEGMENTS - 1):
        pattern = (
            incident
            - jnp.dot(incoming.astype(jnp.bfloat16), coupling, preferred_element_type=jnp.float32)
        ).astype(jnp.bfloat16)
        pattern = jnp.where(my_segment == segment_k, pattern, jnp.zeros_like(pattern))
        make_piece = lax.all_gather(pattern[None], "dom", axis=0, tiled=True)
        count = make_piece.shape[0]
        make_senders = jnp.arange(count, dtype=jnp.int32)
        sender_segment = jnp.sum(
            jnp.where(domain_ids[None, :] == make_senders[:, None], segment_of[None, :], 0), axis=1
        )
        sender_live = sender_segment == segment_k
        match = (
            (partner_row[:, None] == make_senders[None, :])
            & slot_live[:, None]
            & sender_live[None, :]
            & (segment_k < my_segment)
        )
        weights = jnp.sum(
            jnp.where(match[:, :, None, None], trans_rows[:, None, :, :], 0.0), axis=0
        )
        terms = rotate(weights[:, 0][:, None, :], weights[:, 1][:, None, :], make_piece)
        incoming = incoming + jnp.sum(terms, axis=0)
    fields = lax.all_gather(incoming.astype(jnp.bfloat16), "sub", axis=0, tiled=True)
    currents = solved - lax.dot_general(
        spread_half, fields, CONTRACT_LAST, preferred_element_type=jnp.float32
    )
    return currents[None]


def solution(mesh):
    in_specs = (
        P("dom", "sub", None),
        P("dom", "sub", None),
        P("dom", None, "sub"),
        P("dom", "sub", None),
        P("dom", None, None, None),
        P("dom", None),
        P("dom"),
        P(),
    )
    out_specs = P("dom", "sub", None)
    return jax.shard_map(local, mesh=mesh, in_specs=in_specs, out_specs=out_specs, check_vma=False)
```

profile of v0, /device:TPU:0, one launch (start us, length us, event | category | flops | bytes accessed | tf_op | source)
XLA Modules:
  0.0 350.5 jit_solution(12673051462505541044)
XLA Ops:
  6.5 0.0 copy-start
  6.5 0.0 copy-start.3
  6.5 0.0 copy-start.6
  6.5 0.0 copy-start.5
  6.5 0.0 copy-start.4
  6.5 0.0 all-gather.11.cloned.1.call-start
  6.6 0.7 all-gather.11.cloned.1.call-update
  7.3 0.0 reduce-scatter.2.cloned.1.call-start
  7.3 7.1 %all-gather = bf16[1,1536,64]{1,2,0:T(8,128)(2,1)S(1)} all-gather(bf16[1,384,64]{1,2,0:T(8,128)(2,1)} %param.8), channel_id=2, replica_groups=mesh['dom'=8,'sub'=4] {'sub'}, dimensions={1}, use_global_device_ids=true | all-gather | bytes 245760 | tf_op jit(solution)/shard_map/all_gather | solution.py:47
  14.4 0.0 copy-done
  14.4 0.5 fusion.6
  14.9 0.0 copy-done.3
  14.9 1.0 convolution_convert_fusion.1
  15.9 0.0 reduce-scatter.2.cloned.1.call-update
  16.0 0.0 all-reduce.2.cloned.1.call-start
  16.0 0.0 copy-done.6
  16.1 0.6 dynamic_slice.3
  17.9 0.1 select_reduce_fusion.7
  26.5 0.0 copy-done.5
  26.5 0.1 fusion.42
  26.6 0.0 copy-done.4
  26.6 0.2 select_reduce_fusion
  26.8 13.4 %all-gather.11.cloned.1.call-done = bf16[1,1536,1024]{2,1,0:T(8,128)(2,1)} async-done(((bf16[1,384,1024]{2,1,0:T(8,128)(2,1)}), bf16[1,1536,1024]{2,1,0:T(8,128)(2,1)}) %all-gather.11.cloned.1.call-update) | async-done | bytes 3145744 | tf_op jit(solution)/shard_map/all_gather | solution.py:57
  40.2 3.3 fusion.2
  43.5 2.6 convolution_convert_fusion
  46.1 0.0 all-reduce.2.cloned.1.call-update
  46.2 16.0 %reduce-scatter.2.cloned.1.call-done = bf16[16,1024]{1,0:T(8,128)(2,1)} async-done(((bf16[64,1024]{1,0:T(8,128)(2,1)}), bf16[16,1024]{1,0:T(8,128)(2,1)}) %reduce-scatter.2.cloned.1.call-update) | async-done | bytes 32784 | tf_op jit(solution)/shard_map/reduce_scatter | solution.py:49
  62.2 53.9 %all-reduce.2.cloned.1.call-done = bf16[1024,1024]{1,0:T(8,128)(2,1)} async-done(((bf16[1024,1024]{1,0:T(8,128)(2,1)}), bf16[1024,1024]{1,0:T(8,128)(2,1)}) %all-reduce.2.cloned.1.call-update) | async-done | bytes 2097168 | tf_op jit(solution)/shard_map/psum | solution.py:62
  116.1 0.0 copy-start.1
  116.1 0.0 copy-start.2
  116.2 2.1 fusion.10
  118.3 30.8 %all-gather.2 = bf16[128,1024]{1,0:T(8,128)(2,1)S(1)} all-gather(bf16[16,1024]{1,0:T(8,128)(2,1)S(1)} %fusion.10), channel_id=4, replica_groups=mesh['dom'=8,'sub'=4] {'dom'}, dimensions={0}, use_global_device_ids=true | all-gather | bytes 294912 | tf_op jit(solution)/shard_map/all_gather | solution.py:76
  149.1 0.1 multiply_subtract_fusion.6
  149.3 0.0 copy-done.1
  149.3 0.0 copy-done.2
  149.3 0.4 fusion.22
  149.7 30.8 %all-gather.3 = bf16[128,1024]{1,0:T(8,128)(2,1)S(1)} all-gather(bf16[16,1024]{1,0:T(8,128)(2,1)S(1)} %fusion.22), channel_id=5, replica_groups=mesh['dom'=8,'sub'=4] {'dom'}, dimensions={0}, use_global_device_ids=true | all-gather | bytes 294912 | tf_op jit(solution)/shard_map/all_gather | solution.py:76
  180.5 0.1 multiply_subtract_fusion.5
  180.7 0.4 fusion.21
  181.1 30.9 %all-gather.4 = bf16[128,1024]{1,0:T(8,128)(2,1)S(1)} all-gather(bf16[16,1024]{1,0:T(8,128)(2,1)S(1)} %fusion.21), channel_id=6, replica_groups=mesh['dom'=8,'sub'=4] {'dom'}, dimensions={0}, use_global_device_ids=true | all-gather | bytes 294912 | tf_op jit(solution)/shard_map/all_gather | solution.py:76
  212.0 0.1 multiply_subtract_fusion.4
  212.1 0.4 fusion.20
  212.5 30.8 %all-gather.5 = bf16[128,1024]{1,0:T(8,128)(2,1)S(1)} all-gather(bf16[16,1024]{1,0:T(8,128)(2,1)S(1)} %fusion.20), channel_id=7, replica_groups=mesh['dom'=8,'sub'=4] {'dom'}, dimensions={0}, use_global_device_ids=true | all-gather | bytes 294912 | tf_op jit(solution)/shard_map/all_gather | solution.py:76
  243.4 0.1 multiply_subtract_fusion.3
  243.6 0.4 fusion.19
  243.9 30.8 %all-gather.6 = bf16[128,1024]{1,0:T(8,128)(2,1)S(1)} all-gather(bf16[16,1024]{1,0:T(8,128)(2,1)S(1)} %fusion.19), channel_id=8, replica_groups=mesh['dom'=8,'sub'=4] {'dom'}, dimensions={0}, use_global_device_ids=true | all-gather | bytes 294912 | tf_op jit(solution)/shard_map/all_gather | solution.py:76
  274.8 0.1 multiply_subtract_fusion.2
  274.9 0.4 fusion.18
  275.3 30.7 %all-gather.7 = bf16[128,1024]{1,0:T(8,128)(2,1)S(1)} all-gather(bf16[16,1024]{1,0:T(8,128)(2,1)S(1)} %fusion.18), channel_id=9, replica_groups=mesh['dom'=8,'sub'=4] {'dom'}, dimensions={0}, use_global_device_ids=true | all-gather | bytes 294912 | tf_op jit(solution)/shard_map/all_gather | solution.py:76
  306.1 0.1 multiply_subtract_fusion.1
  306.2 0.4 fusion.17
  306.6 30.7 %all-gather.8 = bf16[128,1024]{1,0:T(8,128)(2,1)S(1)} all-gather(bf16[16,1024]{1,0:T(8,128)(2,1)S(1)} %fusion.17), channel_id=10, replica_groups=mesh['dom'=8,'sub'=4] {'dom'}, dimensions={0}, use_global_device_ids=true | all-gather | bytes 294912 | tf_op jit(solution)/shard_map/all_gather | solution.py:76
  337.4 0.1 multiply_subtract_fusion
  337.5 5.4 %all_gather.39 = bf16[64,1024]{1,0:T(8,128)(2,1)S(1)} all-gather(bf16[16,1024]{1,0:T(8,128)(2,1)S(1)} %add_convert_fusion), channel_id=1, replica_groups=mesh['dom'=8,'sub'=4] {'sub'}, dimensions={0}, use_global_device_ids=true | all-gather | bytes 163840 | tf_op jit(solution)/shard_map/all_gather | solution.py:94
  343.0 1.0 fusion.8
  (30 shorter events, 0.6 us)
Async XLA Ops:
  6.5 7.9 %copy-start = (bf16[1,384,1536]{2,1,0:T(8,128)(2,1)S(1)}, bf16[1,384,1536]{2,1,0:T(8,128)(2,1)}, u32[]{:S(2)}) copy-start(bf16[1,384,1536]{2,1,0:T(8,128)(2,1)} %param.9) | copy-start | bytes 3538948
  6.5 8.4 %copy-start.3 = (bf16[1,1024,384]{2,1,0:T(8,128)(2,1)S(1)}, bf16[1,1024,384]{2,1,0:T(8,128)(2,1)}, u32[]{:S(2)}) copy-start(bf16[1,1024,384]{2,1,0:T(8,128)(2,1)} %param.10) | copy-start | bytes 2359300
  6.5 9.5 %copy-start.6 = (s32[8]{0:T(128)S(1)}, s32[8]{0:T(128)}, u32[]{:S(2)}) copy-start(s32[8]{0:T(128)} %param.15) | copy-start | bytes 100
  6.5 20.0 %copy-start.5 = (s32[1,6]{1,0:T(1,128)S(1)}, s32[1,6]{1,0:T(1,128)}, u32[]{:S(2)}) copy-start(s32[1,6]{1,0:T(1,128)} %param.13) | copy-start | bytes 76
  6.5 20.1 %copy-start.4 = (f32[1,6,2,512]{3,2,1,0:T(2,128)S(1)}, f32[1,6,2,512]{3,2,1,0:T(2,128)}, u32[]{:S(2)}) copy-start(f32[1,6,2,512]{3,2,1,0:T(2,128)} %param.12) | copy-start | bytes 73732
  6.5 33.7 %all-gather.11.cloned.1.call-start = ((), (), s32[]{:S(2)}) async-start(), calls=%async_computation.3 | async-start | bytes 3932160 | tf_op jit(solution)/shard_map/all_gather | solution.py:57
  7.3 54.9 %reduce-scatter.2.cloned.1.call-start = ((), (), s32[]{:S(2)}) async-start(), calls=%async_computation.1 | async-start | bytes 163840 | tf_op jit(solution)/shard_map/reduce_scatter | solution.py:49
  16.0 100.2 %all-reduce.2.cloned.1.call-start = ((), (), s32[]{:S(2)}) async-start(), calls=%async_computation.2 | async-start | bytes 4194304 | tf_op jit(solution)/shard_map/psum | solution.py:62
  116.1 33.1 %copy-start.1 = (bf16[1024,1024]{1,0:T(8,128)(2,1)S(1)}, bf16[1024,1024]{1,0:T(8,128)(2,1)}, u32[]{:S(2)}) copy-start(bf16[1024,1024]{1,0:T(8,128)(2,1)} %all-reduce.2.cloned.1.call-done) | copy-start | bytes 6291460
  116.1 33.1 %copy-start.2 = (bf16[16,1024]{1,0:T(8,128)(2,1)S(1)}, bf16[16,1024]{1,0:T(8,128)(2,1)}, u32[]{:S(2)}) copy-start(bf16[16,1024]{1,0:T(8,128)(2,1)} %reduce-scatter.2.cloned.1.call-done) | copy-start | bytes 98308
Sparse Core Ops, SparseCore 0:
  8.9 31.2 all-gather.10
  42.6 19.5 reduce-scatter.1
  64.7 51.3 all-reduce.1
where the time goes:
time: 351 us; the launch traced here: 350 us
  blocking collectives  228 us (65%)
  waiting for transfers between devices  84.1 us (24%)
  between operations  23.2 us (7%)
  matrix products  12.9 us (4%)
    all_gather x7, blocking collectives, local(): make_piece = lax.all_gather(pattern[None], 'dom', axis=0, tiled=True)  216 us
    psum x1, waiting for transfers between devices, local(): coupling = lax.psum(partial_map.astype(jnp.bfloat16), 'sub')  53.9 us
    reduce_scatter x1, waiting for transfers between devices, local(): lax.psum_scatter(lax.dot_general(solved_half, agg_columns, CONTRACT_FIRST...  16 us
    all_gather x1, waiting for transfers between devices, local(): lax.all_gather(disagg_rows, 'sub', axis=0, tiled=True)  13.4 us
    all_gather x1, blocking collectives, local(): lax.all_gather(excite_rows, 'sub', axis=0, tiled=True)  7.08 us
  transfers between devices with their start and end apart: 3, of which 3 were waited for; matrix products, arithmetic and copies ran while one was open for 2% of the time, Pallas kernels for 0%

commit v1 on v0

v1 whole, which is shorter than its diff:
```python
import functools

import jax
import jax.numpy as jnp
from jax import lax
from jax.experimental import pallas as pl
from jax.experimental.pallas import tpu as pltpu
from jax.sharding import PartitionSpec as P

SEGMENTS = 8
CHUNKS = 4
MESH = pl.DeviceIdType.MESH
F32 = jnp.float32
BF16 = jnp.bfloat16


def each(lo, hi, body):
    if hi - lo <= 8:
        for i in range(lo, hi):
            body(i)
    else:
        lax.fori_loop(lo, hi, lambda i, c: (body(i), c)[1], 0)


def kernel(
    n,
    exc_ref, inv_ref, agg_ref, dis_ref, w_ref,
    out_ref,
    exc_all, dis_all, agg_t, solved, inc_part, inc_recv, inc, spread,
    pm, ps_recv, ps, py_recv, coup, pat, recv, field_all,
    exc_s, exc_r, dp_s, dp_r, ds_s, ds_r, dr_s, dr_r, inc_s, inc_r,
    pm_s, pm_r, py_s, py_r, cs_s, cs_r, pat_s, pat_r, fld_s, fld_r,
):
    me = lax.axis_index("dom")
    sub = lax.axis_index("sub")
    core = lax.rem(sub, 2)
    sib = sub + 1 - 2 * core
    peer = lax.rem(sub + 2, 4)
    rows = exc_ref.shape[0]
    wide = dis_ref.shape[1]
    cols = wide // CHUNKS
    half = cols // 2
    rhs = exc_ref.shape[1]
    part = rhs // 4
    q = wide // 2

    barrier = pltpu.get_barrier_semaphore()
    for off in range(1, 4):
        pl.semaphore_signal(barrier, inc=1, device_id={"sub": lax.rem(sub + off, 4)}, device_id_type=MESH)
    each(1, n, lambda off: pl.semaphore_signal(
        barrier, inc=1, device_id={"dom": lax.rem(me + off, n)}, device_id_type=MESH))
    pl.semaphore_wait(barrier, n + 2)

    def to_sub(src, dst, ss, rs, t):
        return pltpu.make_async_remote_copy(
            src_ref=src, dst_ref=dst, send_sem=ss, recv_sem=rs, device_id={"sub": t}, device_id_type=MESH)

    exc_copies = [
        to_sub(exc_ref, exc_all.at[off - 1], exc_s.at[off - 1], exc_r.at[off - 1], lax.rem(sub + off, 4))
        for off in range(1, 4)
    ]
    for c in exc_copies:
        c.start()

    def cut(j):
        return pl.ds(j * cols, cols)

    dp = [to_sub(dis_ref.at[:, cut(j)], dis_all.at[1, :, cut(j)], dp_s.at[j], dp_r.at[j], peer) for j in range(CHUNKS)]
    ds = [to_sub(dis_ref.at[:, cut(j)], dis_all.at[0, :, cut(j)], ds_s.at[j], ds_r.at[j], sib) for j in range(CHUNKS)]
    dr = [to_sub(dis_all.at[1, :, cut(j)], dis_all.at[2, :, cut(j)], dr_s.at[j], dr_r.at[j], sib) for j in range(CHUNKS)]
    for j in range(CHUNKS):
        dp[j].start()
        ds[j].start()

    agg_t[...] = agg_ref[...].T

    def inverse_columns(t):
        return inv_ref[:, pl.ds(pl.multiple_of(t * rows, 128), rows)]

    acc = jnp.dot(inverse_columns(sub), exc_ref[...], preferred_element_type=F32)
    for off in range(1, 4):
        exc_copies[off - 1].wait_recv()
        acc += jnp.dot(inverse_columns(lax.rem(sub + 4 - off, 4)), exc_all[off - 1], preferred_element_type=F32)
    solved[...] = acc
    inc_part[...] = jnp.dot(acc.T.astype(BF16), agg_t[...], preferred_element_type=F32).astype(BF16)

    def inc_rows(t):
        return inc_part.at[pl.ds(pl.multiple_of(t * part, 16), part), :]

    inc_copies = [
        to_sub(inc_rows(lax.rem(sub + off, 4)), inc_recv.at[off - 1], inc_s.at[off - 1], inc_r.at[off - 1], lax.rem(sub + off, 4))
        for off in range(1, 4)
    ]
    for c in inc_copies:
        c.start()

    mine = pl.multiple_of(core * half, half)
    other = pl.multiple_of((1 - core) * half, half)
    pmc = [to_sub(pm.at[j, pl.ds(other, half), :], ps_recv.at[j], pm_s.at[j], pm_r.at[j], sib) for j in range(CHUNKS)]
    pyc = [to_sub(ps.at[j], py_recv.at[j], py_s.at[j], py_r.at[j], peer) for j in range(CHUNKS)]
    own = [coup.at[pl.ds(pl.multiple_of(j * cols + core * half, half), half), :] for j in range(CHUNKS)]
    csc = [to_sub(own[j], own[j], cs_s.at[j], cs_r.at[j], sib) for j in range(CHUNKS)]

    def relay(j):
        dp[j].wait_recv()
        dr[j].start()

    def product(j):
        ds[j].wait_recv()
        dr[j].wait_recv()
        far = sib + 2 - 4 * (sib // 2)
        total = jnp.dot(inverse_columns(sub), dis_ref[:, cut(j)], preferred_element_type=F32)
        total += jnp.dot(inverse_columns(sib), dis_all[0, :, cut(j)], preferred_element_type=F32)
        total += jnp.dot(inverse_columns(peer), dis_all[1, :, cut(j)], preferred_element_type=F32)
        total += jnp.dot(inverse_columns(far), dis_all[2, :, cut(j)], preferred_element_type=F32)
        spread[:, cut(j)] = total.astype(BF16)
        pm[j] = jnp.dot(total.T.astype(BF16), agg_t[...], preferred_element_type=F32).astype(BF16)
        pmc[j].start()

    def pair(j):
        pmc[j].wait_recv()
        ps[j] = (pm[j, pl.ds(mine, half), :].astype(F32) + ps_recv[j].astype(F32)).astype(BF16)
        pyc[j].start()

    def finish(j):
        pyc[j].wait_recv()
        own[j][...] = (ps[j].astype(F32) + py_recv[j].astype(F32)).astype(BF16)
        csc[j].start()

    relay(0)
    for t in range(CHUNKS + 2):
        if t < CHUNKS:
            if t + 1 < CHUNKS:
                product(t)
                relay(t + 1)
            else:
                product(t)
        if 0 <= t - 1 < CHUNKS:
            pair(t - 1)
        if t == 1:
            total = inc_rows(sub)[...].astype(F32)
            for off in range(1, 4):
                inc_copies[off - 1].wait_recv()
                total += inc_recv[off - 1].astype(F32)
            inc[...] = total
            pat[0] = total.astype(BF16)
        if 0 <= t - 2 < CHUNKS:
            finish(t - 2)
    for j in range(CHUNKS):
        csc[j].wait_recv()

    def pattern_copy(slot, off):
        return pltpu.make_async_remote_copy(
            src_ref=pat.at[slot], dst_ref=recv.at[slot, off - 1],
            send_sem=pat_s.at[slot, off - 1], recv_sem=pat_r.at[slot, off - 1],
            device_id={"dom": lax.rem(me + off, n)}, device_id_type=MESH)

    def exchange(slot):
        each(1, n, lambda off: pattern_copy(slot, off).start())

        def term(off):
            pattern_copy(slot, off).wait()
            e = lax.rem(me + n - off, n)
            wr, wi = w_ref[e, 0:1, :], w_ref[e, 1:2, :]
            p = recv[slot, off - 1].astype(F32)
            pr, pi = p[:, :q], p[:, q:]
            return wr * pr - wi * pi, wr * pi + wi * pr

        zero = jnp.zeros((part, q), F32)
        if n <= 8:
            fr, fi = zero, zero
            for off in range(1, n):
                a, b = term(off)
                fr, fi = fr + a, fi + b
        else:
            def body(off, c):
                a, b = term(off)
                return c[0] + a, c[1] + b
            fr, fi = lax.fori_loop(1, n, body, (zero, zero))
        return jnp.concatenate([fr, fi], axis=1).astype(BF16)

    def step(k, carry):
        slot = lax.rem(k, 2)
        field = exchange(slot)
        pat[1 - slot] = (inc[...] - jnp.dot(field, coup[...], preferred_element_type=F32)).astype(BF16)
        return carry

    lax.fori_loop(0, SEGMENTS - 2, step, 0)
    field = exchange((SEGMENTS - 2) % 2)

    def field_rows(t):
        return field_all.at[pl.ds(pl.multiple_of(t * part, 16), part), :]

    field_rows(sub)[...] = field
    fld = [
        to_sub(field_rows(sub), field_rows(sub), fld_s.at[off - 1], fld_r.at[off - 1], lax.rem(sub + off, 4))
        for off in range(1, 4)
    ]
    for c in fld:
        c.start()
    for c in fld:
        c.wait_recv()
    out_ref[...] = solved[...] - lax.dot_general(
        spread[...], field_all[...], (((1,), (1,)), ((), ())), preferred_element_type=F32)

    for c in exc_copies + inc_copies + dp + ds + dr + pmc + pyc + csc + fld:
        c.wait_send()


def local(
    n, excitation, local_inverse, aggregation, disaggregation, translation, partners, list_counts, sweep_order
):
    domains = sweep_order.shape[0]
    segment_of = sweep_order * SEGMENTS // domains
    my_segment = segment_of[lax.axis_index("dom")]
    row = partners[0]
    live = jnp.arange(row.shape[0], dtype=jnp.int32) < list_counts[0]
    ids = jnp.arange(domains, dtype=jnp.int32)
    match = (row[:, None] == ids[None, :]) & live[:, None] & (segment_of < my_segment)[None, :]
    weights = jnp.sum(jnp.where(match[:, :, None, None], translation[0][:, None], 0.0), axis=0)

    rows, rhs = excitation.shape[1:]
    wide = disaggregation.shape[2]
    cols = wide // CHUNKS
    part = rhs // 4
    dma = lambda *s: pltpu.SemaphoreType.DMA(s)
    vm = pl.BlockSpec(memory_space=pltpu.VMEM)
    out = pl.pallas_call(
        functools.partial(kernel, n),
        out_shape=jax.ShapeDtypeStruct((rows, rhs), F32),
        in_specs=[vm] * 5,
        out_specs=vm,
        scratch_shapes=[
            pltpu.VMEM((3, rows, rhs), BF16),
            pltpu.VMEM((3, rows, wide), BF16),
            pltpu.VMEM((rows, wide), BF16),
            pltpu.VMEM((rows, rhs), F32),
            pltpu.VMEM((rhs, wide), BF16),
            pltpu.VMEM((3, part, wide), BF16),
            pltpu.VMEM((part, wide), F32),
            pltpu.VMEM((rows, wide), BF16),
            pltpu.VMEM((CHUNKS, cols, wide), BF16),
            pltpu.VMEM((CHUNKS, cols // 2, wide), BF16),
            pltpu.VMEM((CHUNKS, cols // 2, wide), BF16),
            pltpu.VMEM((CHUNKS, cols // 2, wide), BF16),
            pltpu.VMEM((wide, wide), BF16),
            pltpu.VMEM((2, part, wide), BF16),
            pltpu.VMEM((2, n - 1, part, wide), BF16),
            pltpu.VMEM((rhs, wide), BF16),
            dma(3), dma(3),
            dma(CHUNKS), dma(CHUNKS), dma(CHUNKS), dma(CHUNKS), dma(CHUNKS), dma(CHUNKS),
            dma(3), dma(3),
            dma(CHUNKS), dma(CHUNKS), dma(CHUNKS), dma(CHUNKS), dma(CHUNKS), dma(CHUNKS),
            dma(2, n - 1), dma(2, n - 1),
            dma(3), dma(3),
        ],
        compiler_params=pltpu.CompilerParams(
            collective_id=0, has_side_effects=True, vmem_limit_bytes=48 * 1024 * 1024
        ),
    )(excitation[0], local_inverse[0], aggregation[0], disaggregation[0], weights)
    return out[None]


def solution(mesh):
    in_specs = (
        P("dom", "sub", None),
        P("dom", "sub", None),
        P("dom", None, "sub"),
        P("dom", "sub", None),
        P("dom", None, None, None),
        P("dom", None),
        P("dom"),
        P(),
    )
    out_specs = P("dom", "sub", None)
    return jax.shard_map(
        functools.partial(local, mesh.shape["dom"]),
        mesh=mesh, in_specs=in_specs, out_specs=out_specs, check_vma=False,
    )
```

time: 351 us -> 120 us (0.34)
  blocking collectives: 228 us -> 0 us
  Pallas kernels: 0 us -> 109 us
  waiting for transfers between devices: 84.1 us -> 0 us
  between operations: 23.2 us -> 0.69 us
  matrix products: 12.9 us -> 0 us
  local copies, waits for them, and re-layouts: 0.65 us -> 5.82 us
    all_gather x9 -> x0, blocking collectives: 228 us -> none  [the longest x7 216 us: local(): make_piece = lax.all_gather(pattern[None], 'dom', axis=0, tiled=True)]
    pallas_call x0 -> x1, Pallas kernels: none -> 109 us  [local(): pl.pallas_call(functools.partial(kernel, n), out_shape=jax.ShapeDtypeStru...]
    psum x1 -> x0, waiting for transfers between devices: 53.9 us -> none  [local(): coupling = lax.psum(partial_map.astype(jnp.bfloat16), 'sub')]
    reduce_scatter x1 -> x0, waiting for transfers between devices: 16 us -> none  [local(): lax.psum_scatter(lax.dot_general(solved_half, agg_columns, CONTRACT_FIRST...]
    all_gather x1 -> x0, waiting for transfers between devices: 13.4 us -> none  [local(): lax.all_gather(disagg_rows, 'sub', axis=0, tiled=True)]
    dot_general x12 -> x0, matrix products: 12.9 us -> none  [the longest x7 4.46 us: local(): jnp.dot(incoming.astype(jnp.bfloat16), coupling, preferred_element_type=j...]
    unnamed x14 -> x7, local copies, waits for them, and re-layouts: 0.03 us -> 4.45 us
  transfers between devices with their start and end apart: 3 -> 0, of which waited for: 3 -> 0; matrix products, arithmetic and copies ran while one was open for 2% -> 0% of each run, Pallas kernels for 0% -> 0%
where the time goes in v1:
time: 120 us; the launch traced here: 119 us
  Pallas kernels  109 us (91%)
  local copies, waits for them, and re-layouts  5.82 us (5%)
  other arithmetic  3.54 us (3%)
    pallas_call x1, Pallas kernels, local(): pl.pallas_call(functools.partial(kernel, n), out_shape=jax.ShapeDtypeStru...  109 us
    unnamed x7, local copies, waits for them, and re-layouts  4.45 us

profile of v1, /device:TPU:0, one launch (start us, length us, event | category | flops | bytes accessed | tf_op | source)
XLA Modules:
  0.0 119.2 jit_solution(16812181801998318967)
XLA Ops:
  0.7 0.7 and_select_fusion
  1.3 0.6 dynamic_slice.3
  1.9 1.3 %broadcast_compare_fusion = pred[8]{0:T(512)(128)(4,1)S(1)} fusion(s32[]{:T(128)} %bitcast.6, s32[8]{0:T(128)} %param.15), kind=kLoop, calls=%fused_computation.9 | loop fusion | flops 136 | bytes 44 | tf_op jit(solution)/shard_map/lt | solution.py:219
  3.2 0.7 fusion.1
  4.0 0.8 select_reduce_fusion
  4.8 0.9 copy.11
  5.7 0.0 copy-start
  5.8 1.3 %copy-done = bf16[1,384,1536]{2,1,0:T(8,128)(2,1)S(1)} copy-done((bf16[1,384,1536]{2,1,0:T(8,128)(2,1)S(1)}, bf16[1,384,1536]{2,1,0:T(8,128)(2,1)}, u32[]{:S(2)}) %copy-start) | copy-done | bytes 1179672
  7.0 0.0 copy-start.1
  7.0 1.1 copy-done.1
  8.2 0.0 copy-start.2
  8.2 1.1 copy-done.2
  9.3 109.2 %shard_map.82 = f32[384,64]{1,0:T(8,128)S(1)} custom-call(bf16[384,64]{1,0:T(8,128)(2,1)S(1)} %bitcast.14, bf16[384,1536]{1,0:T(8,128)(2,1)S(1)} %bitcast.10, bf16[1024,384]{1,0:T(8,128)(2,1)S(1)} %bitcast.12, bf16[384,1024]{1,0:T(8,128)(2,1)S(1)} %bitcast.13, f32[8,2,512]{2,1,0:T(2,128)S(1)} %copy.12.w_ref), custom_call_target="tpu_custom_call" | custom-call | tf_op jit(solution)/shard_map/pallas_call | solution.py:228
  118.5 0.8 copy.13
  (2 shorter events, 0.0 us)
Async XLA Ops:
  5.7 1.3 %copy-start = (bf16[1,384,1536]{2,1,0:T(8,128)(2,1)S(1)}, bf16[1,384,1536]{2,1,0:T(8,128)(2,1)}, u32[]{:S(2)}) copy-start(bf16[1,384,1536]{2,1,0:T(8,128)(2,1)} %param.9) | copy-start | bytes 3538948
  7.0 1.1 copy-start.1
  8.2 1.1 copy-start.2

commit v2 on v1

v2 whole, which is shorter than its diff:
```python
import functools

import jax
import jax.numpy as jnp
from jax import lax
from jax.experimental import pallas as pl
from jax.experimental.pallas import tpu as pltpu
from jax.sharding import PartitionSpec as P

SEGMENTS = 8
CHUNKS = 4
MESH = pl.DeviceIdType.MESH
F32 = jnp.float32
BF16 = jnp.bfloat16


def each(lo, hi, body):
    if hi - lo <= 8:
        for i in range(lo, hi):
            body(i)
    else:
        lax.fori_loop(lo, hi, lambda i, c: (body(i), c)[1], 0)


def kernel(
    n,
    exc_ref, inv_hbm, agg_hbm, dis_hbm, trans_ref, partners_ref, count_ref, order_ref,
    out_ref,
    inv_ref, agg_ref, dis_ref,
    exc_all, dis_all, agg_t, solved_t, inc_part, inc_recv, inc, spread_t,
    pm, ps_recv, ps, py_recv, coup, w, facc,
    pat_a, pat_b, xa_recv, xb_recv, merged_a, merged_b, za_recv, zb_recv, field_all,
    load_s,
    exc_s, exc_r, dp_s, dp_r, ds_s, ds_r, dr_s, dr_r, inc_s, inc_r,
    pm_s, pm_r, py_s, py_r, cs_s, cs_r, xa_s, xa_r, xb_s, xb_r, za_s, za_r, zb_s, zb_r, fld_s, fld_r,
):
    me = lax.axis_index("dom")
    sub = lax.axis_index("sub")
    core = lax.rem(sub, 2)
    sib = sub + 1 - 2 * core
    peer = lax.rem(sub + 2, 4)
    rhs, rows = exc_ref.shape
    wide = dis_ref.shape[1]
    cols = wide // CHUNKS
    half = cols // 2
    part = rhs // 4
    q = wide // 2
    members = n // SEGMENTS
    line = n // 2
    fast = lax.rem(me, 2)
    slow = me // 2

    loads = [
        pltpu.make_async_copy(src, dst, load_s.at[i])
        for i, (src, dst) in enumerate([(inv_hbm, inv_ref), (agg_hbm, agg_ref), (dis_hbm, dis_ref)])
    ]
    for c in loads:
        c.start()

    barrier = pltpu.get_barrier_semaphore()
    for off in range(1, 4):
        pl.semaphore_signal(barrier, inc=1, device_id={"sub": lax.rem(sub + off, 4)}, device_id_type=MESH)
    each(1, n, lambda off: pl.semaphore_signal(
        barrier, inc=1, device_id={"dom": lax.rem(me + off, n)}, device_id_type=MESH))
    pl.semaphore_wait(barrier, n + 2)

    def to_sub(src, dst, ss, rs, t):
        return pltpu.make_async_remote_copy(
            src_ref=src, dst_ref=dst, send_sem=ss, recv_sem=rs, device_id={"sub": t}, device_id_type=MESH)

    exc_copies = [
        to_sub(exc_ref, exc_all.at[off - 1], exc_s.at[off - 1], exc_r.at[off - 1], lax.rem(sub + off, 4))
        for off in range(1, 4)
    ]
    for c in exc_copies:
        c.start()

    def cut(j):
        return pl.ds(j * cols, cols)

    dp = [to_sub(dis_hbm.at[:, cut(j)], dis_all.at[1, :, cut(j)], dp_s.at[j], dp_r.at[j], peer) for j in range(CHUNKS)]
    ds = [to_sub(dis_hbm.at[:, cut(j)], dis_all.at[0, :, cut(j)], ds_s.at[j], ds_r.at[j], sib) for j in range(CHUNKS)]
    dr = [to_sub(dis_all.at[1, :, cut(j)], dis_all.at[2, :, cut(j)], dr_s.at[j], dr_r.at[j], sib) for j in range(CHUNKS)]
    for j in range(CHUNKS):
        dp[j].start()
        ds[j].start()

    my_pos = order_ref[me]
    slots = partners_ref.shape[0]
    slot_pos = [jnp.where(l < count_ref[0], order_ref[partners_ref[l]], -1) for l in range(slots)]

    def weigh(p):
        earlier = p // members < my_pos // members
        total = jnp.zeros((2, q), F32)
        for l in range(slots):
            total += jnp.where((slot_pos[l] == p) & earlier, 1.0, 0.0) * trans_ref[l]
        w[p] = total

    each(0, n - members, weigh)

    loads[1].wait()
    agg_t[...] = agg_ref[...].T
    loads[0].wait()
    loads[2].wait()

    def inverse_columns(t):
        return inv_ref[:, pl.ds(pl.multiple_of(t * rows, 128), rows)]

    def apply(block, t):
        return lax.dot_general(block, inverse_columns(t), (((1,), (1,)), ((), ())), preferred_element_type=F32)

    acc = apply(exc_ref[...], sub)
    for off in range(1, 4):
        exc_copies[off - 1].wait_recv()
        acc += apply(exc_all[off - 1], lax.rem(sub + 4 - off, 4))
    solved_t[...] = acc
    inc_part[...] = jnp.dot(acc.astype(BF16), agg_t[...], preferred_element_type=F32).astype(BF16)

    def inc_rows(t):
        return inc_part.at[pl.ds(pl.multiple_of(t * part, 16), part), :]

    inc_copies = [
        to_sub(inc_rows(lax.rem(sub + off, 4)), inc_recv.at[off - 1], inc_s.at[off - 1], inc_r.at[off - 1], lax.rem(sub + off, 4))
        for off in range(1, 4)
    ]
    for c in inc_copies:
        c.start()

    mine = pl.multiple_of(core * half, half)
    other = pl.multiple_of((1 - core) * half, half)
    pmc = [to_sub(pm.at[j, pl.ds(other, half), :], ps_recv.at[j], pm_s.at[j], pm_r.at[j], sib) for j in range(CHUNKS)]
    pyc = [to_sub(ps.at[j], py_recv.at[j], py_s.at[j], py_r.at[j], peer) for j in range(CHUNKS)]
    own = [coup.at[pl.ds(pl.multiple_of(j * cols + core * half, half), half), :] for j in range(CHUNKS)]
    csc = [to_sub(own[j], own[j], cs_s.at[j], cs_r.at[j], sib) for j in range(CHUNKS)]

    def relay(j):
        dp[j].wait_recv()
        dr[j].start()

    def product(j):
        ds[j].wait_recv()
        dr[j].wait_recv()
        far = sib + 2 - 4 * (sib // 2)
        total = jnp.dot(inverse_columns(sub), dis_ref[:, cut(j)], preferred_element_type=F32)
        total += jnp.dot(inverse_columns(sib), dis_all[0, :, cut(j)], preferred_element_type=F32)
        total += jnp.dot(inverse_columns(peer), dis_all[1, :, cut(j)], preferred_element_type=F32)
        total += jnp.dot(inverse_columns(far), dis_all[2, :, cut(j)], preferred_element_type=F32)
        total = total.T.astype(BF16)
        spread_t[cut(j), :] = total
        pm[j] = jnp.dot(total, agg_t[...], preferred_element_type=F32).astype(BF16)
        pmc[j].start()

    def pair(j):
        pmc[j].wait_recv()
        ps[j] = (pm[j, pl.ds(mine, half), :].astype(F32) + ps_recv[j].astype(F32)).astype(BF16)
        pyc[j].start()

    def finish(j):
        pyc[j].wait_recv()
        own[j][...] = (ps[j].astype(F32) + py_recv[j].astype(F32)).astype(BF16)
        csc[j].start()

    def to_dom(src, dst, ss, rs, d):
        return pltpu.make_async_remote_copy(
            src_ref=src, dst_ref=dst, send_sem=ss, recv_sem=rs, device_id={"dom": d}, device_id_type=MESH)

    def short(src, dst, ss, rs, slot):
        return to_dom(src.at[slot], dst.at[slot], ss.at[slot], rs.at[slot], me + 1 - 2 * fast)

    def long(src, dst, ss, rs, slot, off):
        return to_dom(src.at[slot], dst.at[slot, off - 1], ss.at[slot, off - 1], rs.at[slot, off - 1],
                      2 * lax.rem(slow + off, line) + fast)

    xa = functools.partial(short, pat_a, xa_recv, xa_s, xa_r)
    xb = functools.partial(short, merged_b, xb_recv, xb_s, xb_r)
    za = functools.partial(long, merged_a, za_recv, za_s, za_r)
    zb = functools.partial(long, pat_b, zb_recv, zb_s, zb_r)

    def put(dst, slot, k, values):
        place = jnp.full(values.shape, my_pos, jnp.int32)
        for m in range(members):
            dst[slot, m * part:(m + 1) * part, :] = jnp.where(
                place == k * members + m, values, 0.0).astype(BF16)

    def gather(copies, own, recv, slot):
        total = own[slot].astype(F32)
        if line <= 8:
            for off in range(1, line):
                copies(slot, off).wait()
                total += recv[slot, off - 1].astype(F32)
            return total

        def body(off, c):
            copies(slot, off).wait()
            return c + recv[slot, off - 1].astype(F32)
        return lax.fori_loop(1, line, body, total)

    def begin(slot, k, first, second):
        put(pat_a, slot, k, first())
        xa(slot).start()
        put(pat_b, slot, k, second())
        each(1, line, lambda off: zb(slot, off).start())

    def turn_a(slot):
        xa(slot).wait()
        merged_a[slot] = (pat_a[slot].astype(F32) + xa_recv[slot].astype(F32)).astype(BF16)
        each(1, line, lambda off: za(slot, off).start())

    def turn_b(slot):
        merged_b[slot] = gather(zb, pat_b, zb_recv, slot).astype(BF16)
        xb(slot).start()

    def end(slot, k):
        real = gather(za, merged_a, za_recv, slot)
        xb(slot).wait()
        imag = merged_b[slot].astype(F32) + xb_recv[slot].astype(F32)
        fr, fi = facc[0], facc[1]
        for m in range(members):
            wr, wi = w[k * members + m, 0:1, :], w[k * members + m, 1:2, :]
            pr, pi = real[m * part:(m + 1) * part], imag[m * part:(m + 1) * part]
            fr += wr * pr - wi * pi
            fi += wr * pi + wi * pr
        facc[0] = fr
        facc[1] = fi

    def field_now():
        return jnp.concatenate([facc[0], facc[1]], axis=1).astype(BF16)

    facc[...] = jnp.zeros(facc.shape, F32)
    relay(0)
    for t in range(CHUNKS + 2):
        if t < CHUNKS:
            product(t)
            if t + 1 < CHUNKS:
                relay(t + 1)
        if 0 <= t - 1 < CHUNKS:
            pair(t - 1)
        if t == 1:
            total = inc_rows(sub)[...].astype(F32)
            for off in range(1, 4):
                inc_copies[off - 1].wait_recv()
                total += inc_recv[off - 1].astype(F32)
            inc[...] = total
            begin(0, 0, lambda: inc[:, :q], lambda: inc[:, q:])
        if t == 2:
            turn_a(0)
        if t == 3:
            turn_b(0)
        if t == 4:
            end(0, 0)
        if 0 <= t - 2 < CHUNKS:
            finish(t - 2)
    for j in range(CHUNKS):
        csc[j].wait_recv()

    def step(k, carry):
        slot = lax.rem(k, 2)
        field = field_now()

        def columns(lo):
            return inc[:, lo:lo + q] - jnp.dot(field, coup[:, lo:lo + q], preferred_element_type=F32)

        begin(slot, k, lambda: columns(0), lambda: columns(q))
        turn_a(slot)
        turn_b(slot)
        end(slot, k)
        return carry

    lax.fori_loop(1, SEGMENTS - 1, step, 0)
    field = field_now()

    def field_rows(t):
        return field_all.at[pl.ds(pl.multiple_of(t * part, 16), part), :]

    field_rows(sub)[...] = field
    fld = [
        to_sub(field_rows(sub), field_rows(sub), fld_s.at[off - 1], fld_r.at[off - 1], lax.rem(sub + off, 4))
        for off in range(1, 4)
    ]
    for c in fld:
        c.start()
    for c in fld:
        c.wait_recv()
    out_ref[...] = solved_t[...] - jnp.dot(field_all[...], spread_t[...], preferred_element_type=F32)

    for c in exc_copies + inc_copies + dp + ds + dr + pmc + pyc + csc + fld:
        c.wait_send()


def local(
    n, excitation, local_inverse, aggregation, disaggregation, translation, partners, list_counts, sweep_order
):
    rows, rhs = excitation.shape[1:]
    wide = disaggregation.shape[2]
    cols = wide // CHUNKS
    part = rhs // 4
    stack = n // SEGMENTS * part
    line = n // 2
    dma = lambda *s: pltpu.SemaphoreType.DMA(s)
    vm = pl.BlockSpec(memory_space=pltpu.VMEM)
    sm = pl.BlockSpec(memory_space=pltpu.SMEM)
    hbm = pl.BlockSpec(memory_space=pl.ANY)
    out = pl.pallas_call(
        functools.partial(kernel, n),
        out_shape=jax.ShapeDtypeStruct((rhs, rows), F32),
        in_specs=[vm, hbm, hbm, hbm, vm, sm, sm, sm],
        out_specs=vm,
        scratch_shapes=[
            pltpu.VMEM(local_inverse.shape[1:], BF16),
            pltpu.VMEM(aggregation.shape[1:], BF16),
            pltpu.VMEM((rows, wide), BF16),
            pltpu.VMEM((3, rhs, rows), BF16),
            pltpu.VMEM((3, rows, wide), BF16),
            pltpu.VMEM((rows, wide), BF16),
            pltpu.VMEM((rhs, rows), F32),
            pltpu.VMEM((rhs, wide), BF16),
            pltpu.VMEM((3, part, wide), BF16),
            pltpu.VMEM((part, wide), F32),
            pltpu.VMEM((wide, rows), BF16),
            pltpu.VMEM((CHUNKS, cols, wide), BF16),
            pltpu.VMEM((CHUNKS, cols // 2, wide), BF16),
            pltpu.VMEM((CHUNKS, cols // 2, wide), BF16),
            pltpu.VMEM((CHUNKS, cols // 2, wide), BF16),
            pltpu.VMEM((wide, wide), BF16),
            pltpu.VMEM((n, 2, wide // 2), F32),
            pltpu.VMEM((2, part, wide // 2), F32),
            *[pltpu.VMEM((2, stack, wide // 2), BF16)] * 6,
            *[pltpu.VMEM((2, line - 1, stack, wide // 2), BF16)] * 2,
            pltpu.VMEM((rhs, wide), BF16),
            dma(3),
            dma(3), dma(3),
            dma(CHUNKS), dma(CHUNKS), dma(CHUNKS), dma(CHUNKS), dma(CHUNKS), dma(CHUNKS),
            dma(3), dma(3),
            dma(CHUNKS), dma(CHUNKS), dma(CHUNKS), dma(CHUNKS), dma(CHUNKS), dma(CHUNKS),
            dma(2), dma(2), dma(2), dma(2),
            *[dma(2, line - 1)] * 4,
            dma(3), dma(3),
        ],
        compiler_params=pltpu.CompilerParams(
            collective_id=0, has_side_effects=True, vmem_limit_bytes=56 * 1024 * 1024
        ),
    )(
        excitation[0].T, local_inverse[0], aggregation[0], disaggregation[0],
        translation[0], partners[0], list_counts, sweep_order,
    )
    return out.T[None]


def solution(mesh):
    in_specs = (
        P("dom", "sub", None),
        P("dom", "sub", None),
        P("dom", None, "sub"),
        P("dom", "sub", None),
        P("dom", None, None, None),
        P("dom", None),
        P("dom"),
        P(),
    )
    out_specs = P("dom", "sub", None)
    return jax.shard_map(
        functools.partial(local, mesh.shape["dom"]),
        mesh=mesh, in_specs=in_specs, out_specs=out_specs, check_vma=False,
    )
```

time: 120 us -> 102 us (0.85)
  Pallas kernels: 109 us -> 99.8 us
  local copies, waits for them, and re-layouts: 5.82 us -> 1.54 us
  other arithmetic: 3.54 us -> 0 us
    pallas_call x1, Pallas kernels: 109 us -> 99.8 us  [local(): pl.pallas_call(functools.partial(kernel, n), out_shape=jax.ShapeDtypeStru...]
    unnamed x7 -> x1, local copies, waits for them, and re-layouts: 4.45 us -> 1.54 us
    lt x2 -> x0, other arithmetic: 1.32 us -> none  [the longest x1 1.31 us: local(): segment_of < my_segment]
where the time goes in v2:
time: 102 us
  Pallas kernels  99.8 us (98%)
  local copies, waits for them, and re-layouts  1.54 us (2%)
    pallas_call x1, Pallas kernels, local(): pl.pallas_call(functools.partial(kernel, n), out_shape=jax.ShapeDtypeStru...  99.8 us

profile of v2, /device:TPU:0, one launch (start us, length us, event | category | flops | bytes accessed | tf_op | source)
XLA Modules:
  0.0 102.0 jit_solution(2818268277163522764)
XLA Ops:
  0.7 99.8 %shard_map.82 = f32[64,384]{1,0:T(8,128)} custom-call(bf16[64,384]{1,0:T(8,128)(2,1)} %bitcast.15, bf16[384,1536]{1,0:T(8,128)(2,1)} %bitcast.11, bf16[1024,384]{1,0:T(8,128)(2,1)} %bitcast.12, bf16[384,1024]{1,0:T(8,128)(2,1)} %bitcast.13, f32[6,2,512]{2,1,0:T(2,128)} %bitcast.16, s32[6]{0:T(128)} %bitcast.17, s32[1]{0:T(128)S(6)} %copy.10.count_ref, ...), custom_call_target="tpu_custom_call" | custom-call | tf_op jit(solution)/shard_map/pallas_call | solution.py:303
  100.5 1.5 %copy.11 = f32[1,384,64]{1,2,0:T(8,128)} copy(f32[1,384,64]{1,2,0:T(8,128)} %bitcast.14) | data formatting | bytes 196608

commit v3 on v2

--- a/solution.py
+++ b/solution.py
@@ -233,8 +233,7 @@
             product(t)
             if t + 1 < CHUNKS:
                 relay(t + 1)
-        if 0 <= t - 1 < CHUNKS:
-            pair(t - 1)
+            pair(t)
         if t == 1:
             total = inc_rows(sub)[...].astype(F32)
             for off in range(1, 4):

time: 102 us -> 101 us (level)
    pallas_call x1, Pallas kernels: 99.8 us -> 98.8 us  [local(): pl.pallas_call(functools.partial(kernel, n), out_shape=jax.ShapeDtypeStru...]
where the time goes in v3:
time: 101 us
  Pallas kernels  98.8 us (98%)
  local copies, waits for them, and re-layouts  1.54 us (2%)
    pallas_call x1, Pallas kernels, local(): pl.pallas_call(functools.partial(kernel, n), out_shape=jax.ShapeDtypeStru...  98.8 us

profile of v3, /device:TPU:0, one launch (start us, length us, event | category | flops | bytes accessed | tf_op | source)
XLA Modules:
  0.0 101.0 jit_solution(2161579324349883573)
XLA Ops:
  0.7 98.8 %shard_map.82 = f32[64,384]{1,0:T(8,128)} custom-call(bf16[64,384]{1,0:T(8,128)(2,1)} %bitcast.15, bf16[384,1536]{1,0:T(8,128)(2,1)} %bitcast.11, bf16[1024,384]{1,0:T(8,128)(2,1)} %bitcast.12, bf16[384,1024]{1,0:T(8,128)(2,1)} %bitcast.13, f32[6,2,512]{2,1,0:T(2,128)} %bitcast.16, s32[6]{0:T(128)} %bitcast.17, s32[1]{0:T(128)S(6)} %copy.10.count_ref, ...), custom_call_target="tpu_custom_call" | custom-call | tf_op jit(solution)/shard_map/pallas_call | solution.py:302
  99.4 1.5 %copy.11 = f32[1,384,64]{1,2,0:T(8,128)} copy(f32[1,384,64]{1,2,0:T(8,128)} %bitcast.14) | data formatting | bytes 196608
